TPU v7x, 32 devices: a whole 2x2x4 slice. The times are simulated.
32 devices in a mesh: dp: 2 (over core), expert: 16 (over z, y, x).
Axes of the slice: x: 2, y: 2, z: 4, core: 2. Of those that a mesh axis runs over, the one named last changes fastest.
Arguments:
- hidden_in: bfloat16 [32768, 1024], P(('dp', 'expert')), may hold values from -6 to 6
- buckets: int32 [16384, 1], P(('dp', 'expert')), may hold values from 0 to 15; in each aligned block of 512 rows (0 to 511, 512 to 1023, ...) at most 64 rows name the same one
- expert_of_bucket: int32 [16], replicated, may hold values from 0 to 15, each once
- lengths: int32 [32, 3], P(('dp', 'expert')), may hold values from 1 to 384, 512 in all within a row
- norm1_gain: float32 [1024], replicated, may hold values from 0.25 to 1.75
- norm1_bias: float32 [1024], replicated, may hold values from -1.2 to 1.2
- w_qkv: bfloat16 [1024, 3072], replicated, may hold values from -0.1875 to 0.1875
- w_out: bfloat16 [1024, 1024], replicated, may hold values from -0.75 to 0.75
- norm2_gain: float32 [1024], replicated, may hold values from 0.25 to 1.75
- norm2_bias: float32 [1024], replicated, may hold values from -1.2 to 1.2
- w_up: bfloat16 [16, 1024, 4096], P('expert', None, 'dp'), may hold values from -0.1875 to 0.1875
- b_up: float32 [16, 4096], P('expert', 'dp'), may hold values from -1.8 to 1.8
- w_down: bfloat16 [16, 4096, 1024], P('expert', 'dp'), may hold values from -0.09375 to 0.09375
- b_down: float32 [16, 1024], P('expert'), may hold values from -1.8 to 1.8
- grad_out: bfloat16 [32768, 1024], P(('dp', 'expert')), may hold values from -6 to 6
Outputs:
- hidden_out: bfloat16 [32768, 1024], P(('dp', 'expert'))
- grad_in: bfloat16 [32768, 1024], P(('dp', 'expert'))
- grad_qkv: float32 [1024, 3072], P(('dp', 'expert'))
- grad_wout: float32 [1024, 1024], P(('dp', 'expert'))
- grad_norm1_gain: float32 [1024], P(('dp', 'expert'))
- grad_norm1_bias: float32 [1024], P(('dp', 'expert'))
- grad_norm2_gain: float32 [1024], P(('dp', 'expert'))
- grad_norm2_bias: float32 [1024], P(('dp', 'expert'))
- grad_up: float32 [16, 1024, 4096], P('expert', None, 'dp')
- grad_bup: float32 [16, 4096], P('expert', 'dp')
- grad_down: float32 [16, 4096, 1024], P('expert', 'dp')
- grad_bdown: float32 [16, 1024], P('expert', 'dp')
Inputs may be any that keep to these rules, and one draw needn't show every extreme that they name: `buckets`: among the 512 tokens of one device no bucket appears more than 64 times, and in every draw some bucket appears exactly 64 times on some device. `expert_of_bucket`: each expert serves exactly one bucket. `lengths`: each row sums to 512 and its largest entry is 384.
All inputs are finite; a program needn't handle non-finite values.
Results may differ from a plain program's by a relative error of at most 0.014.
Values may be sent and summed in bfloat16 or wider, within the bound.
A program may use at most 192 MiB of HBM per device.

v0:
```python
import jax
import jax.numpy as jnp
from jax import lax
from jax.sharding import PartitionSpec as P

HEADS = 16
HEAD_DIM = 64


norm_eps = 1e-05
masked_score = -1e30
root_half = 0.7071067811865476
inv_root_tau = 0.3989422804014327


def normalize(values):
    mean_val = jnp.mean(values, axis=-1, keepdims=True)
    centered = values - mean_val
    variance = jnp.mean(centered * centered, axis=-1, keepdims=True)
    inv_std = lax.rsqrt(variance + norm_eps)
    return (centered * inv_std, inv_std)


def norm_back(grad_normed, normed, inv_std, gain_vec):
    scaled = grad_normed * gain_vec
    mean_grad = jnp.mean(scaled, axis=-1, keepdims=True)
    mean_cross = jnp.mean(scaled * normed, axis=-1, keepdims=True)
    return inv_std * (scaled - mean_grad - normed * mean_cross)


def gelu_slope(values):
    return 0.5 * (1.0 + lax.erf(values * root_half)) + values * inv_root_tau * jnp.exp(
        -0.5 * values * values
    )


def local_routes(buckets, expert_of_bucket, slot_rows):
    experts_all = expert_of_bucket.shape[0]
    tok_rows = buckets.shape[0]
    capacity = slot_rows // experts_all
    labels = jnp.arange(experts_all, dtype=jnp.int32)
    bucket_hot = (buckets == labels[None, :]).astype(jnp.int32)
    expert_tok = jnp.sum(bucket_hot * expert_of_bucket[None, :], axis=1)
    expert_hot = (expert_tok[:, None] == labels[None, :]).astype(jnp.int32)
    before = jnp.cumsum(expert_hot, axis=0) - expert_hot
    rank_tok = jnp.sum(before * expert_hot, axis=1)
    slot_local = expert_tok * capacity + rank_tok
    source_of_slot = (
        jnp.full((slot_rows,), tok_rows, jnp.int32)
        .at[slot_local]
        .set(jnp.arange(tok_rows, dtype=jnp.int32))
    )
    return (slot_local, source_of_slot)


def to_slots(rows_low, source_of_slot, experts_all):
    model_width = rows_low.shape[1]
    padded = jnp.concatenate([rows_low, jnp.zeros((1, model_width), rows_low.dtype)], axis=0)
    picked = jnp.take(padded, source_of_slot, axis=0)
    return picked.reshape(experts_all, -1, model_width)


def block_scores(query_block, key_rows, allowed, scale_val):
    scores = (
        jnp.einsum("qhd,khd->hqk", query_block, key_rows, preferred_element_type=jnp.float32)
        * scale_val
    )
    return jnp.where(allowed[None], scores, masked_score)


def on_device(
    hidden_in,
    buckets,
    expert_of_bucket,
    lengths,
    norm1_gain,
    norm1_bias,
    w_qkv,
    w_out,
    norm2_gain,
    norm2_bias,
    w_up,
    b_up,
    w_down,
    b_down,
    grad_out,
):
    experts_all = lax.axis_size("expert")
    slot_rows = hidden_in.shape[0]
    model_width = hidden_in.shape[1]
    capacity = slot_rows // experts_all
    tok_rows = buckets.shape[0]
    scale_val = HEAD_DIM ** (-0.5)
    slot_local, source_of_slot = local_routes(buckets, expert_of_bucket, slot_rows)
    taken_flags = (source_of_slot < tok_rows).astype(jnp.bfloat16).reshape(experts_all, capacity)
    arrived = lax.all_to_all(
        hidden_in.reshape(experts_all, capacity, model_width),
        "expert",
        split_axis=0,
        concat_axis=0,
        tiled=True,
    )
    tokens_in = jnp.take(arrived.reshape(slot_rows, model_width), slot_local, axis=0).astype(
        jnp.float32
    )
    seg_ends = jnp.cumsum(lengths[0])
    positions = jnp.arange(tok_rows, dtype=jnp.int32)
    segment = jnp.sum((positions[:, None] >= seg_ends[None, :]).astype(jnp.int32), axis=1)
    normed1, inv_std1 = normalize(tokens_in)
    attn_in = (normed1 * norm1_gain + norm1_bias).astype(jnp.bfloat16)
    proj_qkv = jnp.dot(attn_in, w_qkv, preferred_element_type=jnp.float32).astype(jnp.bfloat16)
    queries = proj_qkv[:, :model_width].reshape(tok_rows, HEADS, HEAD_DIM)
    key_rows = proj_qkv[:, model_width : 2 * model_width].reshape(tok_rows, HEADS, HEAD_DIM)
    values = proj_qkv[:, 2 * model_width :].reshape(tok_rows, HEADS, HEAD_DIM)
    block_rows = min(512, tok_rows)
    block_idx = 0
    row_start = block_idx * block_rows
    allowed = jnp.logical_and(
        positions[None, :] <= positions[row_start : row_start + block_rows, None],
        segment[None, :] == segment[row_start : row_start + block_rows, None],
    )
    scores = block_scores(queries, key_rows, allowed, scale_val)
    top_score = jnp.max(scores, axis=-1, keepdims=True)
    exp_scores = jnp.exp(scores - top_score)
    row_total = jnp.sum(exp_scores, axis=-1, keepdims=True)
    attended = jnp.einsum(
        "hqk,khd->qhd",
        (exp_scores / row_total).astype(jnp.bfloat16),
        values,
        preferred_element_type=jnp.float32,
    )
    outputs = attended.reshape(block_rows, model_width)
    log_totals = [top_score + jnp.log(row_total)]
    allowed_list = [allowed]
    attended_low = outputs.astype(jnp.bfloat16)
    residual_h = tokens_in + jnp.dot(attended_low, w_out, preferred_element_type=jnp.float32)
    sent_h = to_slots(residual_h.astype(jnp.bfloat16), source_of_slot, experts_all)
    expert_part, live_part = (
        lax.all_to_all(sent_h, "expert", split_axis=0, concat_axis=0, tiled=True),
        lax.all_to_all(taken_flags, "expert", split_axis=0, concat_axis=0, tiled=True),
    )
    expert_h = expert_part.reshape(slot_rows, model_width).astype(jnp.float32)
    live_rows = live_part.reshape(slot_rows, 1).astype(jnp.float32)
    normed2, inv_std2 = normalize(expert_h)
    ffn_in = (normed2 * norm2_gain + norm2_bias).astype(jnp.bfloat16)
    grad_rows = (grad_out.astype(jnp.float32) * live_rows).astype(jnp.bfloat16)
    up_half = w_up[0]
    up_bias = b_up[0]
    down_half = w_down[0]
    down_bias = b_down[0]
    up_full, bias_full, down_full = (
        lax.all_gather(up_half, "dp", axis=1, tiled=True),
        lax.all_gather(up_bias.astype(jnp.bfloat16), "dp", axis=0, tiled=True).astype(
            up_bias.dtype
        ),
        lax.all_gather(down_half, "dp", axis=0, tiled=True),
    )
    hidden_pre = jnp.dot(ffn_in, up_full, preferred_element_type=jnp.float32) + bias_full
    hidden_act = jax.nn.gelu(hidden_pre, approximate=False).astype(jnp.bfloat16)
    ffn_out = jnp.dot(hidden_act, down_full, preferred_element_type=jnp.float32) + down_bias
    hidden_pre = jnp.dot(ffn_in, up_full, preferred_element_type=jnp.float32) + bias_full
    hidden_act = jax.nn.gelu(hidden_pre, approximate=False).astype(jnp.bfloat16)
    grad_hidden = jnp.einsum("rd,fd->rf", grad_rows, down_full, preferred_element_type=jnp.float32)
    grad_pre = (grad_hidden * gelu_slope(hidden_pre)).astype(jnp.bfloat16)
    grad_down_full = jnp.einsum(
        "rf,rd->fd", hidden_act, grad_rows, preferred_element_type=jnp.float32
    )
    grad_up_full = jnp.einsum("rd,rf->df", ffn_in, grad_pre, preferred_element_type=jnp.float32)
    grad_bup_full = jnp.sum(grad_pre, axis=0, dtype=jnp.float32)
    grad_bdown_full = jnp.sum(grad_rows, axis=0, dtype=jnp.float32)
    grad_ffn = jnp.einsum("rf,df->rd", grad_pre, up_full, preferred_element_type=jnp.float32)
    grad_up_half, grad_bup_half, grad_down_half, grad_bdown_half = (
        lax.psum_scatter(
            grad_up_full.astype(jnp.bfloat16), "dp", scatter_dimension=1, tiled=True
        ).astype(jnp.float32),
        lax.psum_scatter(
            grad_bup_full.astype(jnp.bfloat16), "dp", scatter_dimension=0, tiled=True
        ).astype(jnp.float32),
        lax.psum_scatter(
            grad_down_full.astype(jnp.bfloat16), "dp", scatter_dimension=0, tiled=True
        ).astype(jnp.float32),
        lax.psum_scatter(
            grad_bdown_full.astype(jnp.bfloat16), "dp", scatter_dimension=0, tiled=True
        ).astype(jnp.float32),
    )
    hidden_out = ((expert_h + ffn_out) * live_rows).astype(jnp.bfloat16)
    grad_gain2 = jnp.sum(grad_ffn * normed2, axis=0)
    grad_bias2 = jnp.sum(grad_ffn, axis=0)
    grad_expert = grad_rows.astype(jnp.float32) + norm_back(grad_ffn, normed2, inv_std2, norm2_gain)
    returned = lax.all_to_all(
        grad_expert.astype(jnp.bfloat16).reshape(experts_all, capacity, model_width),
        "expert",
        split_axis=0,
        concat_axis=0,
        tiled=True,
    )
    grad_h = jnp.take(returned.reshape(slot_rows, model_width), slot_local, axis=0)
    grad_wout = jnp.einsum("td,te->de", attended_low, grad_h, preferred_element_type=jnp.float32)
    grad_attended = (
        jnp.einsum("te,de->td", grad_h, w_out, preferred_element_type=jnp.float32)
        .astype(jnp.bfloat16)
        .reshape(tok_rows, HEADS, HEAD_DIM)
    )
    block_idx = 0
    scores = block_scores(queries, key_rows, allowed_list[block_idx], scale_val)
    attn_probs = jnp.exp(scores - log_totals[block_idx])
    grad_probs = jnp.einsum(
        "qhd,khd->hqk", grad_attended, values, preferred_element_type=jnp.float32
    )
    row_dot = jnp.sum(attn_probs * grad_probs, axis=-1, keepdims=True)
    grad_scores = (attn_probs * (grad_probs - row_dot)).astype(jnp.bfloat16)
    query_grads = (
        jnp.einsum("hqk,khd->qhd", grad_scores, key_rows, preferred_element_type=jnp.float32)
        * scale_val
    )
    grad_keys = (
        jnp.einsum("hqk,qhd->khd", grad_scores, queries, preferred_element_type=jnp.float32)
        * scale_val
    )
    grad_values = jnp.einsum(
        "hqk,qhd->khd",
        attn_probs.astype(jnp.bfloat16),
        grad_attended,
        preferred_element_type=jnp.float32,
    )
    grad_proj = jnp.concatenate(
        [
            query_grads.reshape(tok_rows, model_width),
            grad_keys.reshape(tok_rows, model_width),
            grad_values.reshape(tok_rows, model_width),
        ],
        axis=1,
    ).astype(jnp.bfloat16)
    grad_wqkv = jnp.einsum("td,te->de", attn_in, grad_proj, preferred_element_type=jnp.float32)
    grad_attn = jnp.einsum("te,de->td", grad_proj, w_qkv, preferred_element_type=jnp.float32)
    grad_gain1 = jnp.sum(grad_attn * normed1, axis=0)
    grad_bias1 = jnp.sum(grad_attn, axis=0)
    grad_tokens = grad_h.astype(jnp.float32) + norm_back(grad_attn, normed1, inv_std1, norm1_gain)
    grad_in = lax.all_to_all(
        to_slots(grad_tokens.astype(jnp.bfloat16), source_of_slot, experts_all),
        "expert",
        split_axis=0,
        concat_axis=0,
        tiled=True,
    ).reshape(slot_rows, model_width)
    norm_terms = jnp.stack([grad_gain1, grad_bias1, grad_gain2, grad_bias2], axis=0)
    grad_qkv, grad_wout_part, norm_parts = (
        lax.psum_scatter(grad_wqkv, ("dp", "expert"), scatter_dimension=0, tiled=True),
        lax.psum_scatter(grad_wout, ("dp", "expert"), scatter_dimension=0, tiled=True),
        lax.psum_scatter(norm_terms, ("dp", "expert"), scatter_dimension=1, tiled=True),
    )
    return (
        hidden_out,
        grad_in,
        grad_qkv,
        grad_wout_part,
        norm_parts[0],
        norm_parts[1],
        norm_parts[2],
        norm_parts[3],
        grad_up_half[None],
        grad_bup_half[None],
        grad_down_half[None],
        grad_bdown_half[None],
    )


def solution(mesh):
    return jax.shard_map(
        on_device,
        mesh=mesh,
        in_specs=(
            P(("dp", "expert"), None),
            P(("dp", "expert"), None),
            P(),
            P(("dp", "expert"), None),
            P(),
            P(),
            P(),
            P(),
            P(),
            P(),
            P("expert", None, "dp"),
            P("expert", "dp"),
            P("expert", "dp", None),
            P("expert", None),
            P(("dp", "expert"), None),
        ),
        out_specs=(
            P(("dp", "expert"), None),
            P(("dp", "expert"), None),
            P(("dp", "expert"), None),
            P(("dp", "expert"), None),
            P(("dp", "expert")),
            P(("dp", "expert")),
            P(("dp", "expert")),
            P(("dp", "expert")),
            P("expert", None, "dp"),
            P("expert", "dp"),
            P("expert", "dp", None),
            P("expert", "dp"),
        ),
        check_vma=False,
    )
```

profile of v0, /device:TPU:0, one launch (start us, length us, event | category | flops | bytes accessed | tf_op | source)
XLA Modules:
  0.0 877.2 jit_solution(7601853221873428041)
XLA Ops:
  7.2 8.5 all-to-all-start
  15.8 0.7 all-gather.6.cloned.1.call-update
  16.8 1.1 reduce-window.18
  18.3 2.4 scatter_custom_fusion
  20.8 0.7 reshape.364
  21.8 37.0 %all-to-all-done = bf16[16,64,1024]{2,1,0:T(8,128)(2,1)} async-done(((bf16[16,64,1024]{2,1,0:T(8,128)(2,1)}), bf16[16,64,1024]{2,1,0:T(8,128)(2,1)}, u32[]{:S(2)}, u32[]{:S(2)}) %all-to-all-start) | async-done | bytes 2097184 | tf_op jit(solution)/shard_map/all_to_all | solution.py:96
  58.9 10.1 %all-to-all-start.2 = ((bf16[16,1,64]{2,1,0:T(2,128)(2,1)}), bf16[16,1,64]{2,1,0:T(2,128)(2,1)S(1)}, u32[]{:S(2)}, u32[]{:S(2)}) async-start(bf16[16,1,64]{2,1,0:T(2,128)(2,1)} %reshape.364), calls=%async_computation.2 | async-start | bytes 16384 | tf_op jit(solution)/shard_map/all_to_all | solution.py:140
  69.0 4.6 gather_fusion
  74.6 6.9 convolution_convert_fusion.2
  81.5 1.7 fusion.83
  83.2 2.3 copy.61
  85.5 2.3 copy.60
  87.8 2.3 copy.59
  90.1 9.9 %fusion.85 = (f32[16,512]{1,0:T(8,128)S(1)}, f32[16,512,512]{1,2,0:T(8,128)}) fusion(bf16[512,16,64]{0,2,1:T(8,128)(2,1)} %bitcast.145, bf16[512,16,64]{0,2,1:T(8,128)(2,1)} %bitcast.143, pred[512,512]{0,1:T(8,128)(4,1)S(1)} %fusion.69), kind=kOutput, calls=%fused_computation.153 | convolution fusion | flops 549445632 | bytes 19169280 | tf_op jit(solution)/shard_map/qhd,khd->hqk/dot_general | solution.py:65
  100.0 8.4 fusion.15
  108.4 8.0 fusion.63
  116.4 1.3 fusion.62
  117.8 5.3 gather_fusion.1
  123.1 3.2 broadcast_select_fusion.1
  126.3 7.2 all-to-all-start.1
  133.6 0.7 all-gather.8.cloned.1.call-update
  134.3 1.8 all-gather.1
  136.8 38.7 %all-to-all-done.1 = bf16[16,64,1024]{2,1,0:T(8,128)(2,1)} async-done(((bf16[16,64,1024]{2,1,0:T(8,128)(2,1)}), bf16[16,64,1024]{2,1,0:T(8,128)(2,1)}, u32[]{:S(2)}, u32[]{:S(2)}) %all-to-all-start.1) | async-done | bytes 2097184 | tf_op jit(solution)/shard_map/all_to_all | solution.py:139
  175.5 1.9 convert_reduce_fusion
  177.5 2.3 fusion.29
  179.9 3.7 fusion.36
  183.7 47.9 %fusion.2 = (bf16[1024,4096]{1,0:T(8,128)(2,1)}, f32[1024,4096]{1,0:T(8,128)}) fusion(f32[4096]{0:T(1024)S(1)} %bitcast.165, bf16[1024,1024]{1,0:T(8,128)(2,1)} %fusion.36, bf16[1,1024,4096]{2,1,0:T(8,128)(2,1)} %all-gather.6.cloned.1.call-done), kind=kOutput, calls=%fused_computation.9 | convolution fusion | flops 8866758656 | bytes 35667968 | tf_op jit(solution)/shard_map/dot_general | solution.py:158
  231.7 19.5 %fusion.86 = (bf16[4096]{0:T(1024)(128)(2,1)S(1)}, bf16[1024,4096]{1,0:T(8,128)(2,1)}) fusion(f32[1024,4096]{1,0:T(8,128)} %get-tuple-element.38, f32[4096]{0:T(1024)S(1)} %bitcast.166, bf16[1,4096,1024]{2,1,0:T(8,128)(2,1)} %all-gather.8.cloned.1.call-done, bf16[1024,1024]{1,0:T(8,128)(2,1)} %param.33, f32[1024]{0:T(1024)S(1)} %copy-done.16), kind=kOutput, calls=%fused_computation.154 | convolution fusion | flops 8643407872 | bytes 35680256 | tf_op jit(solution)/shard_map/rd,fd->rf/dot_general | solution.py:163
  251.2 12.8 %fusion.42 = (f32[1024]{0:T(1024)S(1)}, f32[1024]{0:T(1024)S(1)}, f32[1024]{0:T(1024)S(1)}, f32[1024]{0:T(1024)S(1)}, f32[1024,1024]{1,0:T(8,128)S(1)}) fusion(bf16[16,64,1024]{2,1,0:T(8,128)(2,1)} %all-to-all-done.1, f32[1024]{0:T(1024)S(1)} %copy-done.22, f32[1024]{0:T(1024)S(1)} %copy-done.20, f32[1024]{0:T(1024)S(1)} %copy-done.28, ...), kind=kOutput, calls=%fused_computation.71 | convolution fusion | flops 8600416256 | bytes 23097344 | tf_op jit(solution)/shard_map/rf,df->rd/dot_general | solution.py:171
  264.1 4.2 fusion.41
  268.3 9.9 %all-to-all-start.3 = ((bf16[16,64,1024]{2,1,0:T(8,128)(2,1)}), bf16[16,64,1024]{2,1,0:T(8,128)(2,1)}, u32[]{:S(2)}, u32[]{:S(2)}) async-start(bf16[16,64,1024]{2,1,0:T(8,128)(2,1)} %bitcast.151), calls=%async_computation.3 | async-start | bytes 4194304 | tf_op jit(solution)/shard_map/all_to_all | solution.py:190
  278.3 42.6 %all-to-all-done.3 = bf16[16,64,1024]{2,1,0:T(8,128)(2,1)} async-done(((bf16[16,64,1024]{2,1,0:T(8,128)(2,1)}), bf16[16,64,1024]{2,1,0:T(8,128)(2,1)}, u32[]{:S(2)}, u32[]{:S(2)}) %all-to-all-start.3) | async-done | bytes 2097184 | tf_op jit(solution)/shard_map/all_to_all | solution.py:190
  320.9 4.8 gather_fusion.2
  325.7 1.0 copy-done.8
  326.7 2.3 convolution_convert_fusion.3
  329.0 1.5 copy.64
  330.5 8.5 fusion.64
  339.1 11.4 %multiply_reduce_fusion = (f32[16,512]{1,0:T(8,128)S(1)}, f32[16,512,512]{1,2,0:T(8,128)}) fusion(f32[16,512,512]{1,2,0:T(8,128)} %get-tuple-element.36, f32[16,512]{1,0:T(8,128)S(1)} %log_add_fusion, bf16[512,16,64]{0,2,1:T(8,128)(2,1)S(1)} %bitcast.148, bf16[512,16,64]{0,2,1:T(8,128)(2,1)S(1)} %bitcast.153), kind=kOutput, calls=%fused_computation.16 | convolution fusion | flops 549445632 | bytes 35717120 | tf_op jit(solution)/shard_map/qhd,khd->hqk/dot_general | solution.py:207
  350.4 11.8 %multiply_convert_fusion = bf16[16,512,512]{1,2,0:T(8,128)(2,1)S(1)} fusion(f32[16,512,512]{1,2,0:T(8,128)} %get-tuple-element.41, f32[16,512,512]{1,2,0:T(8,128)} %get-tuple-element.36, f32[16,512]{1,0:T(8,128)S(1)} %get-tuple-element.40, f32[16,512]{1,0:T(8,128)S(1)} %log_add_fusion), kind=kLoop, calls=%fused_computation.15 | loop fusion | flops 16777216 | bytes 42008576 | tf_op jit(solution)/shard_map/convert_element_type | solution.py:211
  362.2 2.6 multiply_convert_fusion.2
  364.9 1.5 multiply_convert_fusion.3
  366.5 0.7 slice-done.1
  367.2 5.4 fusion.60
  372.7 1.0 copy.72
  373.8 15.4 %convolution_convert_fusion = bf16[4096,1024]{1,0:T(8,128)(2,1)} fusion(bf16[1024,4096]{1,0:T(8,128)(2,1)} %get-tuple-element.37, bf16[1024,1024]{1,0:T(8,128)(2,1)} %param.33, f32[1024]{0:T(1024)S(1)} %copy-done.16), kind=kOutput, calls=%fused_computation.48 | convolution fusion | flops 8597274624 | bytes 18878464 | tf_op jit(solution)/shard_map/rf,rd->fd/dot_general | solution.py:165
  389.2 14.9 %convolution_convert_fusion.1 = bf16[1024,4096]{1,0:T(8,128)(2,1)} fusion(bf16[1024,1024]{1,0:T(8,128)(2,1)} %fusion.36, bf16[1024,4096]{1,0:T(8,128)(2,1)} %get-tuple-element.44), kind=kOutput, calls=%fused_computation.49 | convolution fusion | flops 8594128896 | bytes 18874368 | tf_op jit(solution)/shard_map/rd,rf->df/dot_general | solution.py:168
  404.2 4.8 fusion.79
  409.4 10.3 %fusion.67 = f32[1024,3072]{1,0:T(8,128)} fusion(bf16[512,1024]{0,1:T(8,128)(2,1)} %bitcast.159, bf16[512,1024]{0,1:T(8,128)(2,1)} %bitcast.161, bf16[512,1024]{0,1:T(8,128)(2,1)} %bitcast.155, f32[1024]{0:T(1024)S(1)} %copy-done.43, f32[1024]{0:T(1024)S(1)} %copy-done.37, f32[512]{0:T(512)S(1)} %copy-done.34, f32[512]{0:T(512)S(1)} %copy-done.24, ...), kind=kOutput, calls=%fused_computation.104 | convolution fusion | flops 3234332672 | bytes 16790016 | tf_op jit(solution)/shard_map/td,te->de/dot_general | solution.py:234
  419.7 2.5 fusion.59
  422.3 5.3 gather_fusion.3
  427.6 3.2 broadcast_select_fusion
  430.8 9.5 %all-to-all-start.4 = ((bf16[16,64,1024]{2,1,0:T(8,128)(2,1)}), bf16[16,64,1024]{2,1,0:T(8,128)(2,1)}, u32[]{:S(2)}, u32[]{:S(2)}) async-start(bf16[16,64,1024]{2,1,0:T(8,128)(2,1)} %bitcast.149), calls=%async_computation.4 | async-start | bytes 4194304 | tf_op jit(solution)/shard_map/all_to_all | solution.py:239
  442.3 2.1 fusion.82
  444.3 3.3 all-reduce.4
  448.9 15.1 %fusion.44 = bf16[1024,1024]{1,0:T(8,128)(2,1)} fusion(bf16[16,64,1024]{2,1,0:T(8,128)(2,1)} %all-to-all-done.1, bf16[1024,4096]{1,0:T(8,128)(2,1)} %get-tuple-element.37, bf16[1,4096,1024]{2,1,0:T(8,128)(2,1)} %all-gather.8.cloned.1.call-done, f32[1024]{0:T(1024)S(1)} %copy-done.16, f32[1024]{0:T(1024)S(1)} %bitcast.182), kind=kOutput, calls=%fused_computation.73 | convolution fusion | flops 8595177472 | bytes 20979712 | tf_op jit(solution)/shard_map/dot_general | solution.py:160
  464.0 53.4 %reduce-scatter.16.cloned.1.call-done = f32[32,4]{1,0:T(8,128)} async-done(((f32[1024,4]{1,0:T(8,128)}), f32[32,4]{1,0:T(8,128)}) %reduce-scatter.16.cloned.1.call-update) | async-done | bytes 528
  517.4 0.9 fusion.84
  520.7 14.7 %reduce-scatter.14.cloned.1.call-done = bf16[2048,1024]{1,0:T(8,128)(2,1)} async-done(((bf16[4096,1024]{1,0:T(8,128)(2,1)}), bf16[2048,1024]{1,0:T(8,128)(2,1)}) %reduce-scatter.14.cloned.1.call-update) | async-done | bytes 4194320 | tf_op jit(solution)/shard_map/reduce_scatter | solution.py:179
  535.3 6.6 bitcast_convert_fusion
  542.0 13.6 %reduce-scatter.12.cloned.1.call-done = bf16[1024,2048]{1,0:T(8,128)(2,1)} async-done(((bf16[1024,4096]{1,0:T(8,128)(2,1)}), bf16[1024,2048]{1,0:T(8,128)(2,1)}) %reduce-scatter.12.cloned.1.call-update) | async-done | bytes 4194320 | tf_op jit(solution)/shard_map/reduce_scatter | solution.py:173
  555.6 6.7 bitcast_convert_fusion.1
  562.2 141.7 %reduce-scatter.10.cloned.1.call-done = f32[32,1024]{1,0:T(8,128)} async-done(((f32[1024,1024]{1,0:T(8,128)}), f32[32,1024]{1,0:T(8,128)}) %reduce-scatter.10.cloned.1.call-update) | async-done | bytes 131088 | tf_op jit(solution)/shard_map/reduce_scatter | solution.py:249
  703.9 163.1 %reduce-scatter.8.cloned.1.call-done = f32[32,3072]{1,0:T(8,128)} async-done(((f32[1024,3072]{1,0:T(8,128)}), f32[32,3072]{1,0:T(8,128)}) %reduce-scatter.8.cloned.1.call-update) | async-done | bytes 393232 | tf_op jit(solution)/shard_map/reduce_scatter | solution.py:248
  867.0 3.1 copy.81
  (157 shorter events, 8.0 us)
Async XLA Ops:
  7.2 109.2 %copy-start = (bf16[1024,1024]{1,0:T(8,128)(2,1)S(1)}, bf16[1024,1024]{1,0:T(8,128)(2,1)}, u32[]{:S(2)}) copy-start(bf16[1024,1024]{1,0:T(8,128)(2,1)} %param.26) | copy-start | bytes 6291460
  7.2 9.3 %copy-start.45 = (s32[1,3]{1,0:T(1,128)S(1)}, s32[1,3]{1,0:T(1,128)}, u32[]{:S(2)}) copy-start(s32[1,3]{1,0:T(1,128)} %param.22) | copy-start | bytes 40
  7.2 9.5 %copy-start.40 = (s32[16]{0:T(128)S(1)}, s32[16]{0:T(128)}, u32[]{:S(2)}) copy-start(s32[16]{0:T(128)} %param.21) | copy-start | bytes 196
  7.2 9.5 %copy-start.39 = (s32[512,1]{0,1:T(1,128)S(1)}, s32[512,1]{0,1:T(1,128)}, u32[]{:S(2)}) copy-start(s32[512,1]{0,1:T(1,128)} %param.20) | copy-start | bytes 6148
  7.2 51.6 %all-to-all-start = ((bf16[16,64,1024]{2,1,0:T(8,128)(2,1)}), bf16[16,64,1024]{2,1,0:T(8,128)(2,1)}, u32[]{:S(2)}, u32[]{:S(2)}) async-start(bf16[16,64,1024]{2,1,0:T(8,128)(2,1)} %bitcast.156), calls=%async_computation | async-start | bytes 4194304 | tf_op jit(solution)/shard_map/all_to_all | solution.py:96
  15.7 167.9 %all-gather.6.cloned.1.call-start = ((), (), s32[]{:S(2)}) async-start(), calls=%async_computation.14 | async-start | bytes 12582912 | tf_op jit(solution)/shard_map/all_gather | solution.py:152
  16.5 58.0 %copy-start.36 = (f32[1024]{0:T(1024)S(1)}, f32[1024]{0:T(1024)}, u32[]{:S(2)}) copy-start(f32[1024]{0:T(1024)} %param.23) | copy-start | bytes 12292
  16.5 58.0 %copy-start.42 = (f32[1024]{0:T(1024)S(1)}, f32[1024]{0:T(1024)}, u32[]{:S(2)}) copy-start(f32[1024]{0:T(1024)} %param.24) | copy-start | bytes 12292
  18.3 98.1 %copy-start.31 = (pred[512]{0:T(512)(128)(4,1)}, pred[512]{0:T(512)(128)(4,1)S(1)}, u32[]{:S(2)}) copy-start(pred[512]{0:T(512)(128)(4,1)S(1)} %get-tuple-element.24) | copy-start | bytes 1540
  20.8 102.3 %copy-start.29 = (pred[1024]{0:T(1024)(128)(4,1)}, pred[1024]{0:T(1024)(128)(4,1)S(1)}, u32[]{:S(2)}) copy-start(pred[1024]{0:T(1024)(128)(4,1)S(1)} %get-tuple-element.34) | copy-start | bytes 3076
  21.5 60.0 %copy-start.25 = (s32[1024]{0:T(1024)}, s32[1024]{0:T(1024)S(1)}, u32[]{:S(2)}) copy-start(s32[1024]{0:T(1024)S(1)} %pad_clamp_fusion) | copy-start | bytes 12292
  21.6 96.2 %copy-start.17 = (s32[1024]{0:T(1024)}, s32[1024]{0:T(1024)S(1)}, u32[]{:S(2)}) copy-start(s32[1024]{0:T(1024)S(1)} %fusion.74) | copy-start | bytes 12292
  58.9 67.5 %all-to-all-start.2 = ((bf16[16,1,64]{2,1,0:T(2,128)(2,1)}), bf16[16,1,64]{2,1,0:T(2,128)(2,1)S(1)}, u32[]{:S(2)}, u32[]{:S(2)}) async-start(bf16[16,1,64]{2,1,0:T(2,128)(2,1)} %reshape.364), calls=%async_computation.2 | async-start | bytes 16384 | tf_op jit(solution)/shard_map/all_to_all | solution.py:140
  73.6 42.8 %copy-start.1 = (bf16[512,1024]{1,0:T(8,128)(2,1)}, bf16[512,1024]{1,0:T(8,128)(2,1)S(1)}, u32[]{:S(2)}) copy-start(bf16[512,1024]{1,0:T(8,128)(2,1)S(1)} %gather_fusion) | copy-start | bytes 3145732
  74.0 7.5 copy-start.23
  74.5 7.0 copy-start.33
  100.0 8.4 copy-start.12
  100.0 8.4 copy-start.6
  108.4 8.0 copy-start.14
  116.4 1.3 copy-start.46
  123.1 11.2 %copy-start.35 = (f32[1,2048]{1,0:T(1,128)S(1)}, f32[1,2048]{1,0:T(1,128)}, u32[]{:S(2)}) copy-start(f32[1,2048]{1,0:T(1,128)} %param.30) | copy-start | bytes 24580
  126.3 53.6 %copy-start.27 = (f32[1024]{0:T(1024)S(1)}, f32[1024]{0:T(1024)}, u32[]{:S(2)}) copy-start(f32[1024]{0:T(1024)} %param.27) | copy-start | bytes 12292
  126.3 53.6 %copy-start.38 = (f32[1024]{0:T(1024)S(1)}, f32[1024]{0:T(1024)}, u32[]{:S(2)}) copy-start(f32[1024]{0:T(1024)} %param.28) | copy-start | bytes 12292
  126.3 49.2 %all-to-all-start.1 = ((bf16[16,64,1024]{2,1,0:T(8,128)(2,1)}), bf16[16,64,1024]{2,1,0:T(8,128)(2,1)}, u32[]{:S(2)}, u32[]{:S(2)}) async-start(bf16[16,64,1024]{2,1,0:T(8,128)(2,1)} %bitcast.150), calls=%async_computation.1 | async-start | bytes 4194304 | tf_op jit(solution)/shard_map/all_to_all | solution.py:139
  133.5 98.1 %all-gather.8.cloned.1.call-start = ((), (), s32[]{:S(2)}) async-start(), calls=%async_computation.15 | async-start | bytes 12582912 | tf_op jit(solution)/shard_map/all_gather | solution.py:156
  177.5 54.1 %copy-start.19 = (f32[1024]{0:T(1024)}, f32[1024]{0:T(1024)S(1)}, u32[]{:S(2)}) copy-start(f32[1024]{0:T(1024)S(1)} %div.39) | copy-start | bytes 12292
  179.9 51.7 %copy-start.21 = (f32[1024]{0:T(1024)}, f32[1024]{0:T(1024)S(1)}, u32[]{:S(2)}) copy-start(f32[1024]{0:T(1024)S(1)} %rsqrt.21) | copy-start | bytes 12292
  183.7 48.0 %copy-start.16 = (f32[1024]{0:T(1024)S(1)}, f32[1024]{0:T(1024)}, u32[]{:S(2)}) copy-start(f32[1024]{0:T(1024)} %reshape.303) | copy-start | bytes 12292
  231.6 19.6 %copy-start.20 = (f32[1024]{0:T(1024)S(1)}, f32[1024]{0:T(1024)}, u32[]{:S(2)}) copy-start(f32[1024]{0:T(1024)} %copy-done.19) | copy-start | bytes 12292
  231.6 19.6 %copy-start.22 = (f32[1024]{0:T(1024)S(1)}, f32[1024]{0:T(1024)}, u32[]{:S(2)}) copy-start(f32[1024]{0:T(1024)} %copy-done.21) | copy-start | bytes 12292
  231.6 19.5 %copy-start.28 = (f32[1024]{0:T(1024)S(1)}, f32[1024]{0:T(1024)}, u32[]{:S(2)}) copy-start(f32[1024]{0:T(1024)} %param.27) | copy-start | bytes 12292
  231.7 19.5 %copy-start.41 = (bf16[1,1024,4096]{2,1,0:T(8,128)(2,1)S(1)}, bf16[1,1024,4096]{2,1,0:T(8,128)(2,1)}, u32[]{:S(2)}) copy-start(bf16[1,1024,4096]{2,1,0:T(8,128)(2,1)} %all-gather.6.cloned.1.call-done) | copy-start | bytes 25165828
  251.2 12.9 %copy-start.5 = (bf16[1024,1024]{1,0:T(8,128)(2,1)S(1)}, bf16[1024,1024]{1,0:T(8,128)(2,1)}, u32[]{:S(2)}) copy-start(bf16[1024,1024]{1,0:T(8,128)(2,1)} %param.33) | copy-start | bytes 6291460
  264.1 14.2 %copy-start.13 = (f32[16,512]{1,0:T(8,128)S(1)}, f32[16,512]{1,0:T(8,128)}, u32[]{:S(2)}) copy-start(f32[16,512]{1,0:T(8,128)} %copy-done.12) | copy-start | bytes 98308
  264.1 14.2 %copy-start.15 = (f32[16,512]{1,0:T(8,128)S(1)}, f32[16,512]{1,0:T(8,128)}, u32[]{:S(2)}) copy-start(f32[16,512]{1,0:T(8,128)} %copy-done.14) | copy-start | bytes 98308
  264.1 56.8 %copy-start.26 = (s32[1024]{0:T(1024)S(1)}, s32[1024]{0:T(1024)}, u32[]{:S(2)}) copy-start(s32[1024]{0:T(1024)} %copy-done.25) | copy-start | bytes 12292
  268.3 58.4 %copy-start.32 = (pred[512]{0:T(512)(128)(4,1)S(1)}, pred[512]{0:T(512)(128)(4,1)}, u32[]{:S(2)}) copy-start(pred[512]{0:T(512)(128)(4,1)} %copy-done.31) | copy-start | bytes 1540
  268.3 52.6 %all-to-all-start.3 = ((bf16[16,64,1024]{2,1,0:T(8,128)(2,1)}), bf16[16,64,1024]{2,1,0:T(8,128)(2,1)}, u32[]{:S(2)}, u32[]{:S(2)}) async-start(bf16[16,64,1024]{2,1,0:T(8,128)(2,1)} %bitcast.151), calls=%async_computation.3 | async-start | bytes 4194304 | tf_op jit(solution)/shard_map/all_to_all | solution.py:190
  278.2 239.2 %reduce-scatter.16.cloned.1.call-start = ((), (), s32[]{:S(2)}) async-start(), calls=%async_computation.16 | async-start | bytes 540672
  325.7 1.0 copy-start.8
  330.5 8.5 copy-start.7
  339.1 27.4 %copy-start.10 = (bf16[16,64,512]{2,1,0:T(8,128)(2,1)}, bf16[16,64,512]{2,1,0:T(8,128)(2,1)S(1)}, u32[]{:S(2)}) copy-start(bf16[16,64,512]{2,1,0:T(8,128)(2,1)S(1)} %fusion.64) | copy-start | bytes 3145732
  350.4 11.8 %copy-start.4 = (bf16[512,1024]{0,1:T(8,128)(2,1)S(1)}, bf16[512,1024]{0,1:T(8,128)(2,1)}, u32[]{:S(2)}) copy-start(bf16[512,1024]{0,1:T(8,128)(2,1)} %copy.60) | copy-start | bytes 3145732
  362.2 2.7 copy-start.3
  362.2 4.2 slice-start
  364.9 1.6 copy-start.11
  364.9 1.6 copy-start.2
  364.9 1.6 copy-start.24
  364.9 1.6 copy-start.34
  364.9 1.6 copy-start.37
  364.9 2.3 slice-start.1
  366.4 6.2 copy-start.9
  373.7 161.6 %reduce-scatter.14.cloned.1.call-start = ((), (), s32[]{:S(2)}) async-start(), calls=%async_computation.13 | async-start | bytes 12582912 | tf_op jit(solution)/shard_map/reduce_scatter | solution.py:179
  389.2 166.4 %reduce-scatter.12.cloned.1.call-start = ((), (), s32[]{:S(2)}) async-start(), calls=%async_computation.12 | async-start | bytes 12582912 | tf_op jit(solution)/shard_map/reduce_scatter | solution.py:173
  404.2 5.2 copy-start.43
  404.2 299.7 %reduce-scatter.10.cloned.1.call-start = ((), (), s32[]{:S(2)}) async-start(), calls=%async_computation.11 | async-start | bytes 4325376 | tf_op jit(solution)/shard_map/reduce_scatter | solution.py:249
  409.0 457.9 %reduce-scatter.8.cloned.1.call-start = ((), (), s32[]{:S(2)}) async-start(), calls=%async_computation.10 | async-start | bytes 12976128 | tf_op jit(solution)/shard_map/reduce_scatter | solution.py:248
  419.6 2.6 copy-start.18
  422.3 5.4 copy-start.30
  427.6 12.7 %copy-start.47 = (u32[32]{0:T(128)S(1)}, u32[32]{0:T(128)}, u32[]{:S(2)}) copy-start(u32[32]{0:T(128)} %constant.138) | copy-start | bytes 388
  427.6 21.3 %copy-start.44 = (f32[1,1024]{1,0:T(1,128)S(1)}, f32[1,1024]{1,0:T(1,128)}, u32[]{:S(2)}) copy-start(f32[1,1024]{1,0:T(1,128)} %param.32) | copy-start | bytes 12292
  430.8 89.9 %all-to-all-start.4 = ((bf16[16,64,1024]{2,1,0:T(8,128)(2,1)}), bf16[16,64,1024]{2,1,0:T(8,128)(2,1)}, u32[]{:S(2)}, u32[]{:S(2)}) async-start(bf16[16,64,1024]{2,1,0:T(8,128)(2,1)} %bitcast.149), calls=%async_computation.4 | async-start | bytes 4194304 | tf_op jit(solution)/shard_map/all_to_all | solution.py:239
Sparse Core Ops, SparseCore 0:
  18.1 21.0 all-gather.5
  135.9 21.0 all-gather.7
  373.9 143.5 reduce-scatter.15
  519.7 15.6 reduce-scatter.13
  537.5 18.0 reduce-scatter.11
  558.4 145.4 reduce-scatter.9
  711.5 155.3 reduce-scatter.7
where the time goes:
time: 881 us; the launch traced here: 877 us
  waiting for transfers between devices  506 us (57%)
  matrix products  198 us (22%)
  other arithmetic  60.6 us (7%)
  starting transfers between devices  45.9 us (5%)
  local copies, waits for them, and re-layouts  44.4 us (5%)
  between operations  16.6 us (2%)
    reduce_scatter x1, waiting for transfers between devices, on_device(): lax.psum_scatter(grad_wqkv, ('dp', 'expert'), scatter_dimension=0, tiled=...  163 us
    reduce_scatter x1, waiting for transfers between devices, on_device(): lax.psum_scatter(grad_wout, ('dp', 'expert'), scatter_dimension=0, tiled=...  142 us
    unnamed x8, waiting for transfers between devices  54.9 us
    dot_general x1, matrix products, on_device(): jnp.dot(ffn_in, up_full, preferred_element_type=jnp.float32) + bias_full  47.9 us
    all_to_all x1, waiting for transfers between devices, on_device(): lax.all_to_all(grad_expert.astype(jnp.bfloat16).reshape(experts_all, capa...  42.6 us
    all_to_all x1, waiting for transfers between devices, on_device(): lax.all_to_all(sent_h, 'expert', split_axis=0, concat_axis=0, tiled=True)  38.7 us
    all_to_all x1, waiting for transfers between devices, on_device(): lax.all_to_all(hidden_in.reshape(experts_all, capacity, model_width), 'ex...  37 us
    dot_general x1, matrix products, on_device(): jnp.einsum('rd,fd->rf', grad_rows, down_full, preferred_element_type=jnp....  19.5 us
  transfers between devices with their start and end apart: 12, of which 8 were waited for; matrix products, arithmetic and copies ran while one was open for 24% of the time, Pallas kernels for 0%

commit v1 on v0

--- a/solution.py
+++ b/solution.py
@@ -1,6 +1,10 @@
+import functools
+
 import jax
 import jax.numpy as jnp
 from jax import lax
+from jax.experimental import pallas as pl
+from jax.experimental.pallas import tpu as pltpu
 from jax.sharding import PartitionSpec as P
 
 HEADS = 16
@@ -66,6 +70,370 @@
         * scale_val
     )
     return jnp.where(allowed[None], scores, masked_score)
+
+
+MESH_ID = pl.DeviceIdType.MESH
+PARTS = 4
+UNITS = 256
+
+
+def mm(a, b):
+    return jnp.dot(a, b, preferred_element_type=jnp.float32)
+
+
+def mm_nt(a, b):
+    return lax.dot_general(a, b, (((1,), (1,)), ((), ())), preferred_element_type=jnp.float32)
+
+
+def mm_tn(a, b):
+    return lax.dot_general(a, b, (((0,), (0,)), ((), ())), preferred_element_type=jnp.float32)
+
+
+def gelu_parts(pre):
+    bell = jnp.exp(-0.5 * pre * pre)
+    den = 1.0 + (0.3275911 * root_half) * jnp.abs(pre)
+    t = pl.reciprocal(den, approx=True)
+    t = t * (2.0 - den * t)
+    tail = t * (
+        0.5 * 0.254829592
+        + t * (0.5 * -0.284496736 + t * (0.5 * 1.421413741 + t * (0.5 * -1.453152027 + t * (0.5 * 1.061405429))))
+    )
+    tail = tail * bell
+    phi = jnp.where(pre >= 0.0, 1.0 - tail, tail)
+    return pre * phi, phi + pre * (inv_root_tau * bell)
+
+
+def greet(me_d, me_e, n):
+    barrier = pltpu.get_barrier_semaphore()
+
+    def signal(i, carry):
+        pl.semaphore_signal(barrier, inc=1, device_id=(me_d, me_e ^ i), device_id_type=MESH_ID)
+        return carry
+
+    lax.fori_loop(1, n, signal, 0)
+    pl.semaphore_signal(barrier, inc=1, device_id=(1 - me_d, me_e), device_id_type=MESH_ID)
+    pl.semaphore_wait(barrier, n)
+
+
+def expert_kernel(
+    n,
+    cap,
+    sent,
+    grads,
+    live,
+    up_hbm,
+    up_bias,
+    down_hbm,
+    down_bias,
+    gain,
+    bias,
+    returned,
+    hidden_out,
+    grad_up,
+    grad_down,
+    grad_bup,
+    grad_bdown,
+    grad_norm,
+    rows_in,
+    ffn_in,
+    grad_rows,
+    up,
+    down,
+    act,
+    pre_grad,
+    pre_tile,
+    hid_tile,
+    part_out,
+    part_in,
+    back,
+    tile,
+    tile_down,
+    sem_send,
+    sem_recv,
+    sem_back_send,
+    sem_back_recv,
+    sem_pair,
+    sem_load,
+    sem_store,
+):
+    me_d = lax.axis_index("dp")
+    me_e = lax.axis_index("expert")
+    rows = rows_in.shape[0]
+    width = rows_in.shape[1]
+    units = up.shape[1]
+    block = rows // PARTS
+    many = n // PARTS
+    partner = (1 - me_d, me_e)
+
+    def base_of(part):
+        return pl.multiple_of(((me_e // many) ^ part) * block, block)
+
+    def slot_copy(i):
+        peer = me_e ^ i
+        return pltpu.make_async_remote_copy(
+            src_ref=sent.at[pl.ds(pl.multiple_of(peer * cap, cap), cap)],
+            dst_ref=rows_in.at[pl.ds(pl.multiple_of(me_e * cap, cap), cap)],
+            send_sem=sem_send.at[i],
+            recv_sem=sem_recv.at[i],
+            device_id=(me_d, peer),
+            device_id_type=MESH_ID,
+        )
+
+    def own_slots():
+        own = pl.ds(pl.multiple_of(me_e * cap, cap), cap)
+        return pltpu.make_async_copy(sent.at[own], rows_in.at[own], sem_recv.at[0])
+
+    def back_copy(i):
+        peer = me_e ^ i
+        return pltpu.make_async_remote_copy(
+            src_ref=back.at[pl.ds(pl.multiple_of(peer * cap, cap), cap)],
+            dst_ref=returned.at[pl.ds(pl.multiple_of(me_e * cap, cap), cap)],
+            send_sem=sem_back_send.at[i],
+            recv_sem=sem_back_recv.at[i],
+            device_id=(me_d, peer),
+            device_id_type=MESH_ID,
+        )
+
+    def own_back():
+        own = pl.ds(pl.multiple_of(me_e * cap, cap), cap)
+        return pltpu.make_async_copy(back.at[own], returned.at[own], sem_back_recv.at[0])
+
+    def pair_copy(src, dst, kind, part):
+        return pltpu.make_async_remote_copy(
+            src_ref=src,
+            dst_ref=dst,
+            send_sem=sem_pair.at[kind, 0, part],
+            recv_sem=sem_pair.at[kind, 1, part],
+            device_id=partner,
+            device_id_type=MESH_ID,
+        )
+
+    def grads_pair(part):
+        return pair_copy(
+            grads.at[pl.ds(base_of(part), block)], grad_rows.at[part, pl.ds(block, block)], 0, part
+        )
+
+    def ffn_pair(part):
+        return pair_copy(
+            ffn_in.at[part, pl.ds(0, block)], ffn_in.at[part, pl.ds(block, block)], 1, part
+        )
+
+    def part_pair(part):
+        return pair_copy(part_out.at[part], part_in.at[part], 2, part)
+
+    def out_pair(part):
+        return pair_copy(part_out.at[PARTS + part], part_in.at[PARTS + part], 3, part)
+
+    def grads_load(part):
+        return pltpu.make_async_copy(
+            grads.at[pl.ds(base_of(part), block)], grad_rows.at[part, pl.ds(0, block)], sem_load.at[2 + part]
+        )
+
+    up_load = pltpu.make_async_copy(up_hbm, up, sem_load.at[0])
+    down_load = pltpu.make_async_copy(down_hbm, down, sem_load.at[1])
+
+    greet(me_d, me_e, n)
+    own_slots().start()
+    for part in range(PARTS):
+        grads_pair(part).start()
+        grads_load(part).start()
+    down_load.start()
+    up_load.start()
+
+    def start_slots(i, carry):
+        slot_copy(i).start()
+        return carry
+
+    lax.fori_loop(1, n, start_slots, 0)
+    grad_norm[...] = jnp.zeros_like(grad_norm)
+    down_load.wait()
+    up_load.wait()
+
+    def stats(base):
+        x = rows_in[pl.ds(base, block), :].astype(jnp.float32)
+        return normalize(x)
+
+    def work(part, carry):
+        base = base_of(part)
+
+        @pl.when(part == 0)
+        def _():
+            own_slots().wait()
+
+        @pl.when(part > 0)
+        def _():
+            slot_copy(part * many).wait()
+
+        def wait_slots(j, c):
+            slot_copy(part * many + j).wait()
+            return c
+
+        lax.fori_loop(1, many, wait_slots, 0)
+        normed, _ = stats(base)
+        ffn_in[part, 0:block, :] = (normed * gain[...] + bias[...]).astype(jnp.bfloat16)
+        ffn_pair(part).start()
+        grads_load(part).wait()
+        grads_pair(part).wait()
+        ffn_pair(part).wait()
+
+        def hidden(f, c):
+            cols = pl.ds(pl.multiple_of(f * UNITS, UNITS), UNITS)
+            pre = mm(ffn_in[part], up[:, cols]) + up_bias[:, cols]
+            hid = mm_nt(grad_rows[part], down[cols, :])
+            a, slope = gelu_parts(pre)
+            act[part, :, cols] = a.astype(jnp.bfloat16)
+            pre_grad[part, :, cols] = (hid * slope).astype(jnp.bfloat16)
+            return c
+
+        lax.fori_loop(0, units // UNITS, hidden, 0)
+        part_out[part] = mm_nt(pre_grad[part, block:, :], up[...]).astype(jnp.bfloat16)
+        part_pair(part).start()
+        mine = mm_nt(pre_grad[part, 0:block, :], up[...])
+        part_pair(part).wait()
+        grad_ffn = mine + part_in[part].astype(jnp.float32)
+        normed, inv_std = stats(base)
+        grad_norm[0:1, :] += jnp.sum(grad_ffn * normed, axis=0, keepdims=True)
+        grad_norm[1:2, :] += jnp.sum(grad_ffn, axis=0, keepdims=True)
+        result = grad_rows[part, 0:block, :].astype(jnp.float32) + norm_back(
+            grad_ffn, normed, inv_std, gain[...]
+        )
+        back[pl.ds(base, block), :] = result.astype(jnp.bfloat16)
+
+        @pl.when(part == 0)
+        def _():
+            own_back().start()
+
+        @pl.when(part > 0)
+        def _():
+            back_copy(part * many).start()
+
+        def start_back(j, c):
+            back_copy(part * many + j).start()
+            return c
+
+        lax.fori_loop(1, many, start_back, 0)
+        return carry
+
+    lax.fori_loop(0, PARTS, work, 0)
+
+    def output(part, carry):
+        part_out[PARTS + part] = mm(act[part, block:, :], down[...]).astype(jnp.bfloat16)
+        out_pair(part).start()
+        return carry
+
+    lax.fori_loop(0, PARTS, output, 0)
+
+    def output_own(part, carry):
+        base = base_of(part)
+        here = pl.ds(base, block)
+        mine = mm(act[part, 0:block, :], down[...])
+        out_pair(part).wait()
+        total = rows_in[here, :].astype(jnp.float32) + mine + part_in[PARTS + part].astype(jnp.float32) + down_bias[...]
+        rows_in[here, :] = (total * live[here, :]).astype(jnp.bfloat16)
+        pltpu.make_async_copy(rows_in.at[here], hidden_out.at[here], sem_store.at[part]).start()
+        return carry
+
+    lax.fori_loop(0, PARTS, output_own, 0)
+
+    ones = jnp.ones((8, PARTS * 2 * block), jnp.bfloat16)
+    all_act = act.reshape(PARTS * 2 * block, units)
+    all_pre = pre_grad.reshape(PARTS * 2 * block, units)
+    all_in = ffn_in.reshape(PARTS * 2 * block, width)
+    all_grad = grad_rows.reshape(PARTS * 2 * block, width)
+    grad_bup[...] = mm(ones, all_pre[...])
+    grad_bdown[...] = mm(ones, all_grad[...])
+
+    def up_store(f, slot):
+        cols = pl.ds(pl.multiple_of(f * UNITS, UNITS), UNITS)
+        return pltpu.make_async_copy(tile.at[slot], grad_up.at[:, cols], sem_store.at[PARTS + slot])
+
+    def down_store(f, slot):
+        cols = pl.ds(pl.multiple_of(f * UNITS, UNITS), UNITS)
+        return pltpu.make_async_copy(
+            tile_down.at[slot], grad_down.at[cols, :], sem_store.at[PARTS + 2 + slot]
+        )
+
+    def weights(f, carry):
+        slot = lax.rem(f, 2)
+        cols = pl.ds(pl.multiple_of(f * UNITS, UNITS), UNITS)
+
+        @pl.when(f >= 2)
+        def _():
+            up_store(f, slot).wait()
+            down_store(f, slot).wait()
+
+        tile[slot] = mm_tn(all_in[...], all_pre[:, cols])
+        up_store(f, slot).start()
+        tile_down[slot] = mm_tn(all_act[:, cols], all_grad[...])
+        down_store(f, slot).start()
+        return carry
+
+    lax.fori_loop(0, units // UNITS, weights, 0)
+    for slot in range(2):
+        up_store(0, slot).wait()
+        down_store(0, slot).wait()
+    for part in range(PARTS):
+        pltpu.make_async_copy(
+            rows_in.at[pl.ds(0, block)], hidden_out.at[pl.ds(0, block)], sem_store.at[part]
+        ).wait()
+    own_back().wait()
+
+    def wait_back(i, carry):
+        back_copy(i).wait()
+        return carry
+
+    lax.fori_loop(1, n, wait_back, 0)
+
+
+def expert_block(sent, grads, live, up, up_bias, down, down_bias, gain, bias):
+    n = lax.axis_size("expert")
+    rows, width = sent.shape
+    units = up.shape[1]
+    cap = rows // n
+    block = rows // PARTS
+    vm = pl.BlockSpec(memory_space=pltpu.VMEM)
+    hbm = pl.BlockSpec(memory_space=pl.ANY)
+    f32, low = jnp.float32, jnp.bfloat16
+    return pl.pallas_call(
+        functools.partial(expert_kernel, n, cap),
+        out_shape=(
+            jax.ShapeDtypeStruct((rows, width), low),
+            jax.ShapeDtypeStruct((rows, width), low),
+            jax.ShapeDtypeStruct((width, units), f32),
+            jax.ShapeDtypeStruct((units, width), f32),
+            jax.ShapeDtypeStruct((8, units), f32),
+            jax.ShapeDtypeStruct((8, width), f32),
+            jax.ShapeDtypeStruct((8, width), f32),
+        ),
+        in_specs=[hbm, hbm, vm, hbm, vm, hbm, vm, vm, vm],
+        out_specs=(hbm, hbm, hbm, hbm, vm, vm, vm),
+        scratch_shapes=[
+            pltpu.VMEM((rows, width), low),
+            pltpu.VMEM((PARTS, 2 * block, width), low),
+            pltpu.VMEM((PARTS, 2 * block, width), low),
+            pltpu.VMEM((width, units), low),
+            pltpu.VMEM((units, width), low),
+            pltpu.VMEM((PARTS, 2 * block, units), low),
+            pltpu.VMEM((PARTS, 2 * block, units), low),
+            pltpu.VMEM((2, 2 * block, UNITS), f32),
+            pltpu.VMEM((2, 2 * block, UNITS), f32),
+            pltpu.VMEM((2 * PARTS, block, width), low),
+            pltpu.VMEM((2 * PARTS, block, width), low),
+            pltpu.VMEM((rows, width), low),
+            pltpu.VMEM((2, width, UNITS), f32),
+            pltpu.VMEM((2, UNITS, width), f32),
+            pltpu.SemaphoreType.DMA((n,)),
+            pltpu.SemaphoreType.DMA((n,)),
+            pltpu.SemaphoreType.DMA((n,)),
+            pltpu.SemaphoreType.DMA((n,)),
+            pltpu.SemaphoreType.DMA((4, 2, PARTS)),
+            pltpu.SemaphoreType.DMA((2 + PARTS,)),
+            pltpu.SemaphoreType.DMA((PARTS + 4,)),
+        ],
+        compiler_params=pltpu.CompilerParams(
+            collective_id=1, has_side_effects=True, vmem_limit_bytes=60 * 1024 * 1024
+        ),
+    )(sent, grads, live, up, up_bias, down, down_bias, gain, bias)
 
 
 def on_device(
@@ -135,65 +503,32 @@
     attended_low = outputs.astype(jnp.bfloat16)
     residual_h = tokens_in + jnp.dot(attended_low, w_out, preferred_element_type=jnp.float32)
     sent_h = to_slots(residual_h.astype(jnp.bfloat16), source_of_slot, experts_all)
-    expert_part, live_part = (
-        lax.all_to_all(sent_h, "expert", split_axis=0, concat_axis=0, tiled=True),
-        lax.all_to_all(taken_flags, "expert", split_axis=0, concat_axis=0, tiled=True),
-    )
-    expert_h = expert_part.reshape(slot_rows, model_width).astype(jnp.float32)
+    live_part = lax.all_to_all(taken_flags, "expert", split_axis=0, concat_axis=0, tiled=True)
     live_rows = live_part.reshape(slot_rows, 1).astype(jnp.float32)
-    normed2, inv_std2 = normalize(expert_h)
-    ffn_in = (normed2 * norm2_gain + norm2_bias).astype(jnp.bfloat16)
     grad_rows = (grad_out.astype(jnp.float32) * live_rows).astype(jnp.bfloat16)
-    up_half = w_up[0]
-    up_bias = b_up[0]
-    down_half = w_down[0]
-    down_bias = b_down[0]
-    up_full, bias_full, down_full = (
-        lax.all_gather(up_half, "dp", axis=1, tiled=True),
-        lax.all_gather(up_bias.astype(jnp.bfloat16), "dp", axis=0, tiled=True).astype(
-            up_bias.dtype
-        ),
-        lax.all_gather(down_half, "dp", axis=0, tiled=True),
-    )
-    hidden_pre = jnp.dot(ffn_in, up_full, preferred_element_type=jnp.float32) + bias_full
-    hidden_act = jax.nn.gelu(hidden_pre, approximate=False).astype(jnp.bfloat16)
-    ffn_out = jnp.dot(hidden_act, down_full, preferred_element_type=jnp.float32) + down_bias
-    hidden_pre = jnp.dot(ffn_in, up_full, preferred_element_type=jnp.float32) + bias_full
-    hidden_act = jax.nn.gelu(hidden_pre, approximate=False).astype(jnp.bfloat16)
-    grad_hidden = jnp.einsum("rd,fd->rf", grad_rows, down_full, preferred_element_type=jnp.float32)
-    grad_pre = (grad_hidden * gelu_slope(hidden_pre)).astype(jnp.bfloat16)
-    grad_down_full = jnp.einsum(
-        "rf,rd->fd", hidden_act, grad_rows, preferred_element_type=jnp.float32
-    )
-    grad_up_full = jnp.einsum("rd,rf->df", ffn_in, grad_pre, preferred_element_type=jnp.float32)
-    grad_bup_full = jnp.sum(grad_pre, axis=0, dtype=jnp.float32)
-    grad_bdown_full = jnp.sum(grad_rows, axis=0, dtype=jnp.float32)
-    grad_ffn = jnp.einsum("rf,df->rd", grad_pre, up_full, preferred_element_type=jnp.float32)
-    grad_up_half, grad_bup_half, grad_down_half, grad_bdown_half = (
-        lax.psum_scatter(
-            grad_up_full.astype(jnp.bfloat16), "dp", scatter_dimension=1, tiled=True
-        ).astype(jnp.float32),
-        lax.psum_scatter(
-            grad_bup_full.astype(jnp.bfloat16), "dp", scatter_dimension=0, tiled=True
-        ).astype(jnp.float32),
-        lax.psum_scatter(
-            grad_down_full.astype(jnp.bfloat16), "dp", scatter_dimension=0, tiled=True
-        ).astype(jnp.float32),
-        lax.psum_scatter(
-            grad_bdown_full.astype(jnp.bfloat16), "dp", scatter_dimension=0, tiled=True
-        ).astype(jnp.float32),
-    )
-    hidden_out = ((expert_h + ffn_out) * live_rows).astype(jnp.bfloat16)
-    grad_gain2 = jnp.sum(grad_ffn * normed2, axis=0)
-    grad_bias2 = jnp.sum(grad_ffn, axis=0)
-    grad_expert = grad_rows.astype(jnp.float32) + norm_back(grad_ffn, normed2, inv_std2, norm2_gain)
-    returned = lax.all_to_all(
-        grad_expert.astype(jnp.bfloat16).reshape(experts_all, capacity, model_width),
-        "expert",
-        split_axis=0,
-        concat_axis=0,
-        tiled=True,
-    )
+    (
+        returned,
+        hidden_out,
+        grad_up_half,
+        grad_down_half,
+        grad_bup,
+        grad_bdown,
+        grad_norm2,
+    ) = expert_block(
+        sent_h.reshape(slot_rows, model_width),
+        grad_rows,
+        live_rows,
+        w_up[0],
+        b_up,
+        w_down[0],
+        b_down,
+        norm2_gain[None],
+        norm2_bias[None],
+    )
+    grad_bup_half = grad_bup[0]
+    half = model_width // lax.axis_size("dp")
+    grad_bdown_half = lax.dynamic_slice_in_dim(grad_bdown[0], lax.axis_index("dp") * half, half)
+    grad_gain2, grad_bias2 = grad_norm2[0], grad_norm2[1]
     grad_h = jnp.take(returned.reshape(slot_rows, model_width), slot_local, axis=0)
     grad_wout = jnp.einsum("td,te->de", attended_low, grad_h, preferred_element_type=jnp.float32)
     grad_attended = (

time: 881 us -> 781 us (0.89)
  matrix products: 198 us -> 72.3 us
  Pallas kernels: 0 us -> 119 us
  waiting for transfers between devices: 506 us -> 448 us
  starting transfers between devices: 45.9 us -> 11.2 us
  other arithmetic: 60.6 us -> 35.8 us
  local copies, waits for them, and re-layouts: 44.4 us -> 60.4 us
  blocking collectives: 5.11 us -> 15.4 us
    dot_general x6 -> x0, matrix products: 126 us -> none  [the longest x1 47.9 us: on_device(): jnp.dot(ffn_in, up_full, preferred_element_type=jnp.float32) + bias_full]
    pallas_call x0 -> x1, Pallas kernels: none -> 119 us  [expert_block(): pl.pallas_call(functools.partial(expert_kernel, n, cap), out_shape=(jax.S...]
    all_to_all x3 -> x0, waiting for transfers between devices: 81.2 us -> none  [the longest x1 42.6 us: on_device(): lax.all_to_all(grad_expert.astype(jnp.bfloat16).reshape(experts_all, capa...]
    unnamed x8 -> x4, waiting for transfers between devices: 54.9 us -> 108 us
    reduce_scatter x2 -> x0, waiting for transfers between devices: 28.3 us -> none  [the longest x1 14.7 us: on_device(): lax.psum_scatter(grad_down_full.astype(jnp.bfloat16), 'dp', scatter_dimen...]
    all_to_all x3 -> x0, starting transfers between devices: 27.3 us -> none  [the longest x1 10.1 us: on_device(): lax.all_to_all(taken_flags, 'expert', split_axis=0, concat_axis=0, tiled=...]
    all_to_all x0 -> x1, blocking collectives: none -> 15.4 us  [on_device(): lax.all_to_all(taken_flags, 'expert', split_axis=0, concat_axis=0, tiled=...]
    broadcast_in_dim x4 -> x0, other arithmetic: 14.5 us -> none  [the longest x1 6.65 us: on_device(): grad_up_half[None]]
  transfers between devices with their start and end apart: 12 -> 5, of which waited for: 8 -> 4; matrix products, arithmetic and copies ran while one was open for 24% -> 5% of each run, Pallas kernels for 0% -> 0%
where the time goes in v1:
time: 781 us; the launch traced here: 777 us
  waiting for transfers between devices  448 us (57%)
  Pallas kernels  119 us (15%)
  matrix products  72.3 us (9%)
  local copies, waits for them, and re-layouts  60.4 us (8%)
  other arithmetic  35.8 us (5%)
  blocking collectives  15.4 us (2%)
  between operations  14.4 us (2%)
  starting transfers between devices  11.2 us (1%)
    reduce_scatter x1, waiting for transfers between devices, on_device(): lax.psum_scatter(grad_wqkv, ('dp', 'expert'), scatter_dimension=0, tiled=...  160 us
    reduce_scatter x1, waiting for transfers between devices, on_device(): lax.psum_scatter(grad_wout, ('dp', 'expert'), scatter_dimension=0, tiled=...  143 us
    pallas_call x1, Pallas kernels, expert_block(): pl.pallas_call(functools.partial(expert_kernel, n, cap), out_shape=(jax.S...  119 us
    unnamed x4, waiting for transfers between devices  108 us
    all_to_all x1, waiting for transfers between devices, on_device(): lax.all_to_all(hidden_in.reshape(experts_all, capacity, model_width), 'ex...  37 us
    unnamed x49, local copies, waits for them, and re-layouts  21.1 us
  transfers between devices with their start and end apart: 5, of which 4 were waited for; matrix products, arithmetic and copies ran while one was open for 5% of the time, Pallas kernels for 0%

profile of v1, /device:TPU:0, one launch (start us, length us, event | category | flops | bytes accessed | tf_op | source)
XLA Modules:
  0.0 776.5 jit_solution(17094493408814491693)
XLA Ops:
  7.2 0.9 select_reduce_fusion
  8.1 1.1 reduce-window.18
  9.3 0.2 slice_reduce_fusion
  9.5 0.1 fusion.31
  9.7 2.4 scatter_custom_fusion
  12.2 0.1 reshape.307
  12.2 15.4 %all_to_all.24 = bf16[16,1,64]{2,1,0:T(2,128)(2,1)S(1)} all-to-all(bf16[16,1,64]{2,1,0:T(2,128)(2,1)S(1)} %reshape.307), channel_id=1, replica_groups=mesh['dp'=2,'expert'=16] {'expert'}, dimensions={0} | all-to-all | bytes 4096 | tf_op jit(solution)/shard_map/all_to_all | solution.py:506
  27.6 4.6 all-to-all-start
  32.2 0.2 reduce-window.20
  32.4 0.1 convert_reduce_fusion.1
  32.5 0.2 fusion.28
  32.8 1.3 reshape.308.live
  34.1 3.3 multiply_convert_fusion.1.grads
  37.4 37.0 %all-to-all-done = bf16[16,64,1024]{2,1,0:T(8,128)(2,1)} async-done(((bf16[16,64,1024]{2,1,0:T(8,128)(2,1)}), bf16[16,64,1024]{2,1,0:T(8,128)(2,1)}, u32[]{:S(2)}, u32[]{:S(2)}) %all-to-all-start) | async-done | bytes 2097184 | tf_op jit(solution)/shard_map/all_to_all | solution.py:464
  74.5 4.8 gather_fusion
  79.3 0.4 convert_reduce_fusion
  79.6 0.5 fusion.20
  80.2 6.9 convolution_convert_fusion
  87.1 1.7 fusion.41
  88.8 2.3 copy.73
  91.1 2.3 copy.72
  93.4 2.3 copy.71
  95.7 9.9 %fusion.43 = (f32[16,512]{1,0:T(8,128)S(1)}, f32[16,512,512]{1,2,0:T(8,128)}) fusion(bf16[512,16,64]{0,2,1:T(8,128)(2,1)} %bitcast.79, bf16[512,16,64]{0,2,1:T(8,128)(2,1)} %bitcast.77, pred[512,512]{0,1:T(8,128)(4,1)S(1)} %fusion.28), kind=kOutput, calls=%fused_computation.89 | convolution fusion | flops 549445632 | bytes 19169280 | tf_op jit(solution)/shard_map/qhd,khd->hqk/dot_general | solution.py:69
  105.6 8.4 %fusion = f32[16,512]{1,0:T(8,128)S(1)} fusion(f32[16,512,512]{1,2,0:T(8,128)} %get-tuple-element.44, f32[16,512]{1,0:T(8,128)S(1)} %get-tuple-element.43), kind=kLoop, calls=%fused_computation.11 | loop fusion | flops 8380416 | bytes 16842752 | tf_op jit(solution)/shard_map/reduce_sum | solution.py:493
  114.0 7.8 fusion.22
  121.7 1.3 fusion.21
  123.0 0.1 concatenate.10
  123.1 5.3 gather_fusion.1
  128.5 3.2 broadcast_select_fusion.1.sent
  131.6 118.7 %shard_map.238 = (bf16[1024,1024]{1,0:T(8,128)(2,1)}, bf16[1024,1024]{1,0:T(8,128)(2,1)}, f32[1024,2048]{1,0:T(8,128)}, f32[2048,1024]{1,0:T(8,128)}, f32[8,2048...) custom-call(bf16[1024,1024]{1,0:T(8,128)(2,1)} %broadcast_select_fusion.1.sent, ...), custom_call_target="tpu_custom_call" | custom-call | tf_op jit(solution)/shard_map/pallas_call | solution.py:397
  250.3 5.0 gather_fusion.2
  255.3 2.3 convolution_convert_fusion.1
  257.6 1.5 copy.77
  259.1 8.5 %fusion.23 = bf16[16,64,512]{2,1,0:T(8,128)(2,1)S(1)} fusion(bf16[512,16,64]{0,2,1:T(8,128)(2,1)S(1)} %bitcast.81, f32[16,512,512]{1,2,0:T(8,128)} %get-tuple-element.44, f32[16,512]{1,0:T(8,128)S(1)} %log_add_fusion), kind=kOutput, calls=%fused_computation.45 | convolution fusion | flops 545783808 | bytes 18907136 | tf_op jit(solution)/shard_map/hqk,qhd->khd/dot_general | solution.py:555
  267.7 11.4 %multiply_reduce_fusion = (f32[16,512]{1,0:T(8,128)S(1)}, f32[16,512,512]{1,2,0:T(8,128)}) fusion(f32[16,512,512]{1,2,0:T(8,128)} %get-tuple-element.44, f32[16,512]{1,0:T(8,128)S(1)} %log_add_fusion, bf16[512,16,64]{0,2,1:T(8,128)(2,1)S(1)} %bitcast.82, bf16[512,16,64]{0,2,1:T(8,128)(2,1)S(1)} %bitcast.91), kind=kOutput, calls=%fused_computation.6 | convolution fusion | flops 549445632 | bytes 35717120 | tf_op jit(solution)/shard_map/qhd,khd->hqk/dot_general | solution.py:542
  279.1 11.8 %multiply_convert_fusion = bf16[16,512,512]{1,2,0:T(8,128)(2,1)S(1)} fusion(f32[16,512,512]{1,2,0:T(8,128)} %get-tuple-element.46, f32[16,512,512]{1,2,0:T(8,128)} %get-tuple-element.44, f32[16,512]{1,0:T(8,128)S(1)} %get-tuple-element.45, f32[16,512]{1,0:T(8,128)S(1)} %log_add_fusion), kind=kLoop, calls=%fused_computation.5 | loop fusion | flops 16777216 | bytes 42008576 | tf_op jit(solution)/shard_map/convert_element_type | solution.py:546
  290.9 2.6 multiply_convert_fusion.2
  293.6 1.5 multiply_convert_fusion.3
  295.1 0.8 slice.43
  295.9 5.5 fusion.19
  301.4 1.0 copy.85
  302.5 0.2 reduce-scatter.8.cloned.1.call-start
  302.7 4.6 fusion.38
  307.3 1.1 copy-done.9
  308.5 10.0 %fusion.26 = f32[1024,3072]{1,0:T(8,128)} fusion(bf16[512,1024]{0,1:T(8,128)(2,1)} %bitcast.97, bf16[512,1024]{0,1:T(8,128)(2,1)} %bitcast.99, bf16[512,1024]{0,1:T(8,128)(2,1)S(1)} %bitcast.93, f32[1024]{0:T(1024)S(1)} %copy-done.13, f32[1024]{0:T(1024)S(1)} %copy-done.12, f32[512]{0:T(512)S(1)} %add_rsqrt_fusion, f32[512]{0:T(512)S(1)} %broadcast_multiply_fusion.2, ...), kind=kOutput, calls=%fused_computation.46 | convolution fusion | flops 3234332672 | bytes 16790016 | tf_op jit(solution)/shard_map/td,te->de/dot_general | solution.py:569
  318.6 2.3 fusion.18
  321.0 5.3 gather_fusion.3
  326.3 3.2 broadcast_select_fusion
  329.5 6.4 all-to-all-start.2
  335.9 0.8 slice.49
  336.7 1.4 slice.48
  338.1 0.6 constant_dynamic-slice_fusion
  338.7 108.3 %reduce-scatter.10.cloned.1.call-done = f32[32,4]{1,0:T(8,128)} async-done(((f32[1024,4]{1,0:T(8,128)}), f32[32,4]{1,0:T(8,128)}) %reduce-scatter.10.cloned.1.call-update) | async-done | bytes 528
  447.0 0.9 fusion.42
  448.0 0.6 copy.90
  448.5 0.6 copy.89
  449.1 0.6 copy.88
  449.7 0.6 copy.87
  450.3 143.0 %reduce-scatter.8.cloned.1.call-done = f32[32,1024]{1,0:T(8,128)} async-done(((f32[1024,1024]{1,0:T(8,128)}), f32[32,1024]{1,0:T(8,128)}) %reduce-scatter.8.cloned.1.call-update) | async-done | bytes 131088 | tf_op jit(solution)/shard_map/reduce_scatter | solution.py:584
  593.3 160.0 %reduce-scatter.6.cloned.1.call-done = f32[32,3072]{1,0:T(8,128)} async-done(((f32[1024,3072]{1,0:T(8,128)}), f32[32,3072]{1,0:T(8,128)}) %reduce-scatter.6.cloned.1.call-update) | async-done | bytes 393232 | tf_op jit(solution)/shard_map/reduce_scatter | solution.py:583
  753.3 3.1 copy.97
  756.4 1.3 copy.98
  757.7 8.6 %copy.99 = f32[1,1024,2048]{2,1,0:T(8,128)} copy(f32[1,1024,2048]{2,1,0:T(8,128)} %bitcast.86) | data formatting | bytes 16777216
  766.3 3.5 copy.100
  (66 shorter events, 0.6 us)
Async XLA Ops:
  7.2 114.6 %copy-start = (bf16[1024,1024]{1,0:T(8,128)(2,1)S(1)}, bf16[1024,1024]{1,0:T(8,128)(2,1)}, u32[]{:S(2)}) copy-start(bf16[1024,1024]{1,0:T(8,128)(2,1)} %param.26) | copy-start | bytes 6291460
  27.6 4.6 copy-start.14
  27.6 46.8 %all-to-all-start = ((bf16[16,64,1024]{2,1,0:T(8,128)(2,1)}), bf16[16,64,1024]{2,1,0:T(8,128)(2,1)}, u32[]{:S(2)}, u32[]{:S(2)}) async-start(bf16[16,64,1024]{2,1,0:T(8,128)(2,1)} %bitcast.94), calls=%async_computation | async-start | bytes 4194304 | tf_op jit(solution)/shard_map/all_to_all | solution.py:464
  32.2 414.8 %reduce-scatter.10.cloned.1.call-start = ((), (), s32[]{:S(2)}) async-start(), calls=%async_computation.8 | async-start | bytes 540672
  79.2 42.5 %copy-start.2 = (bf16[512,1024]{1,0:T(8,128)(2,1)}, bf16[512,1024]{1,0:T(8,128)(2,1)S(1)}, u32[]{:S(2)}) copy-start(bf16[512,1024]{1,0:T(8,128)(2,1)S(1)} %gather_fusion) | copy-start | bytes 3145732
  79.2 0.9 copy-start.12
  79.2 0.9 copy-start.13
  105.6 8.4 %copy-start.6 = (bf16[512,1024]{0,1:T(8,128)(2,1)S(1)}, bf16[512,1024]{0,1:T(8,128)(2,1)}, u32[]{:S(2)}) copy-start(bf16[512,1024]{0,1:T(8,128)(2,1)} %copy.71) | copy-start | bytes 3145732
  121.7 1.3 copy-start.15
  259.1 8.5 %copy-start.7 = (bf16[512,1024]{0,1:T(8,128)(2,1)S(1)}, bf16[512,1024]{0,1:T(8,128)(2,1)}, u32[]{:S(2)}) copy-start(bf16[512,1024]{0,1:T(8,128)(2,1)} %copy.71) | copy-start | bytes 3145732
  267.7 28.2 %copy-start.10 = (bf16[16,64,512]{2,1,0:T(8,128)(2,1)}, bf16[16,64,512]{2,1,0:T(8,128)(2,1)S(1)}, u32[]{:S(2)}) copy-start(bf16[16,64,512]{2,1,0:T(8,128)(2,1)S(1)} %fusion.23) | copy-start | bytes 3145732
  279.1 11.8 %copy-start.5 = (bf16[512,1024]{0,1:T(8,128)(2,1)S(1)}, bf16[512,1024]{0,1:T(8,128)(2,1)}, u32[]{:S(2)}) copy-start(bf16[512,1024]{0,1:T(8,128)(2,1)} %copy.72) | copy-start | bytes 3145732
  290.9 2.7 copy-start.4
  290.9 5.0 slice-start.2
  293.5 2.3 copy-start.11
  293.6 2.3 copy-start.3
  293.6 2.3 slice-start.3
  295.0 6.3 copy-start.8
  302.5 290.8 %reduce-scatter.8.cloned.1.call-start = ((), (), s32[]{:S(2)}) async-start(), calls=%async_computation.7 | async-start | bytes 4325376 | tf_op jit(solution)/shard_map/reduce_scatter | solution.py:584
  307.2 1.2 copy-start.9
  307.3 446.0 %reduce-scatter.6.cloned.1.call-start = ((), (), s32[]{:S(2)}) async-start(), calls=%async_computation.6 | async-start | bytes 12976128 | tf_op jit(solution)/shard_map/reduce_scatter | solution.py:583
  329.5 120.8 %all-to-all-start.2 = ((bf16[16,64,1024]{2,1,0:T(8,128)(2,1)}), bf16[16,64,1024]{2,1,0:T(8,128)(2,1)S(1)}, u32[]{:S(2)}, u32[]{:S(2)}) async-start(bf16[16,64,1024]{2,1,0:T(8,128)(2,1)} %bitcast.25), calls=%async_computation.2 | async-start | bytes 4194304 | tf_op jit(solution)/shard_map/all_to_all | solution.py:574
  756.4 9.9 %slice-start = ((s8[8388608]{0:T(1024)(128)(4,1)}), s8[4194304]{0:T(1024)(128)(4,1)S(1)}, s32[]{:S(2)}) async-start(s8[8388608]{0:T(1024)(128)(4,1)} %bitcast.83), calls=%async_computation.9 | async-start | bytes 8388608
  757.7 8.6 %slice-start.1 = ((s8[8388608]{0:T(1024)(128)(4,1)}), s8[4194304]{0:T(1024)(128)(4,1)S(1)}, s32[]{:S(2)}) async-start(s8[8388608]{0:T(1024)(128)(4,1)} %bitcast.83), calls=%async_computation.10 | async-start | bytes 8388608
  766.3 3.5 copy-start.1
Sparse Core Ops, SparseCore 0:
  302.6 144.3 reduce-scatter.9
  450.5 142.7 reduce-scatter.7
  600.9 152.3 reduce-scatter.5
